TPU v7x, 256 devices: a whole 4x4x8 slice. The times are simulated.
256 devices in a mesh: rep: 4 (over x), ep: 64 (over y, z, core).
Axes of the slice: x: 4, y: 4, z: 8, core: 2. Of those that a mesh axis runs over, the one named last changes fastest.
Arguments:
- d_out: bfloat16 [32768, 2048], P(('rep', 'ep')), may hold values from -6 to 6
- saved_input: bfloat16 [32768, 2048], P(('rep', 'ep')), may hold values from -6 to 6
- routes: int32 [32768, 6], P(('rep', 'ep')), may hold values from 0 to 63, all different within a row; in each aligned block of 128 rows (0 to 127, 128 to 255, ...) at most 13 rows name the same one
- probs: bfloat16 [32768, 6], P(('rep', 'ep')), may hold values from 0.049804688 to 0.5
- gate_pre: bfloat16 [212992, 704], P(('rep', 'ep')), may hold values from -6 to 6
- up_pre: bfloat16 [212992, 704], P(('rep', 'ep')), may hold values from -6 to 6
- gate_weight: bfloat16 [64, 704, 2048], P('ep', 'rep'), may hold values from -0.125 to 0.125
- up_weight: bfloat16 [64, 704, 2048], P('ep', 'rep'), may hold values from -0.125 to 0.125
- down_weight: bfloat16 [64, 704, 2048], P('ep', 'rep'), may hold values from -0.21875 to 0.21875
Outputs:
- d_tokens: bfloat16 [32768, 2048], P(('rep', 'ep'))
- d_probs: bfloat16 [32768, 6], P(('rep', 'ep'))
- gate_weight_grad: float32 [64, 704, 2048], P('ep', 'rep')
- up_weight_grad: float32 [64, 704, 2048], P('ep', 'rep')
- down_weight_grad: float32 [64, 704, 2048], P('ep', 'rep')
Inputs may be any that keep to these rules, and one draw needn't show every extreme that they name: `routes`: each row names 6 different experts. Among the 128 rows of one device no expert is named more than 13 times, and in some device's rows one expert is named exactly 13 times.
All inputs are finite; a program needn't handle non-finite values.
Results may differ from a plain program's by a relative error of at most 0.012.
Values may be sent and summed in bfloat16 or wider, within the bound.
A program may use at most 128 MiB of HBM per device.

v0:
```python
import jax
import jax.numpy as jnp
from jax import lax
from jax.sharding import PartitionSpec as P


def contract_rows(left, right):
    return lax.dot_general(
        left, right, (((0,), (0,)), ((), ())), preferred_element_type=jnp.float32
    )


def contract_cols(left, right):
    return lax.dot_general(
        left, right, (((1,), (1,)), ((), ())), preferred_element_type=jnp.float32
    )


def on_device(
    d_out, saved_input, routes, probs, gate_pre, up_pre, gate_weight, up_weight, down_weight
):
    experts = lax.axis_size("ep")
    slot_count = gate_pre.shape[0]
    capacity = slot_count // experts
    token_rows = d_out.shape[0]
    chosen = routes.shape[1]
    width = d_out.shape[1]
    flat_ids = routes.reshape(-1)
    route_total = flat_ids.shape[0]
    onehot = (flat_ids[:, None] == jnp.arange(experts, dtype=jnp.int32)[None, :]).astype(jnp.int32)
    running = jnp.cumsum(onehot, axis=0) - 1
    position = jnp.sum(running * onehot, axis=1)
    target = flat_ids * capacity + position
    slot_owner = (
        jnp.full((slot_count,), route_total, jnp.int32)
        .at[target]
        .set(jnp.arange(route_total, dtype=jnp.int32))
    )
    token_id = slot_owner // chosen
    grad_ext = jnp.concatenate([d_out, jnp.zeros((1, width), jnp.bfloat16)], axis=0)
    input_ext = jnp.concatenate([saved_input, jnp.zeros((1, width), jnp.bfloat16)], axis=0)
    prob_ext = jnp.concatenate([probs.reshape(-1), jnp.zeros((1,), jnp.bfloat16)], axis=0)
    send_grad = grad_ext[token_id]
    send_input = input_ext[token_id]
    send_weight = prob_ext[slot_owner]
    slot_grad, slot_input, slot_weight = (
        lax.all_to_all(send_grad, "ep", split_axis=0, concat_axis=0, tiled=True),
        lax.all_to_all(send_input, "ep", split_axis=0, concat_axis=0, tiled=True),
        lax.all_to_all(send_weight, "ep", split_axis=0, concat_axis=0, tiled=True),
    )
    gate_full, up_full, down_full = (
        lax.all_gather(gate_weight, "rep", axis=1, tiled=True),
        lax.all_gather(up_weight, "rep", axis=1, tiled=True),
        lax.all_gather(down_weight, "rep", axis=1, tiled=True),
    )
    gate_full = gate_full[0]
    up_full = up_full[0]
    down_full = down_full[0]
    weight = slot_weight.astype(jnp.float32)
    down_back = contract_cols(slot_grad, down_full)
    gate_val = gate_pre.astype(jnp.float32)
    up_val = up_pre.astype(jnp.float32)
    logistic = jax.nn.sigmoid(gate_val)
    silu_gate = gate_val * logistic
    activation = (silu_gate * up_val).astype(jnp.bfloat16)
    prob_grad = jnp.sum(down_back * activation.astype(jnp.float32), axis=1).astype(jnp.bfloat16)
    weighted_grad = (weight[:, None] * slot_grad.astype(jnp.float32)).astype(jnp.bfloat16)
    down_part = contract_rows(activation, weighted_grad)[None]
    scaled = weight[:, None] * down_back
    gate_back = (scaled * up_val * logistic * (1.0 + gate_val * (1.0 - logistic))).astype(
        jnp.bfloat16
    )
    up_back = (scaled * silu_gate).astype(jnp.bfloat16)
    input_grad = (
        jnp.dot(gate_back, gate_full, preferred_element_type=jnp.float32)
        + jnp.dot(up_back, up_full, preferred_element_type=jnp.float32)
    ).astype(jnp.bfloat16)
    returned_grad, returned_prob = (
        lax.all_to_all(input_grad, "ep", split_axis=0, concat_axis=0, tiled=True),
        lax.all_to_all(prob_grad, "ep", split_axis=0, concat_axis=0, tiled=True),
    )
    gate_part = contract_rows(gate_back, slot_input)[None]
    up_part = contract_rows(up_back, slot_input)[None]
    gate_grad, up_grad, down_grad = (
        lax.psum_scatter(
            gate_part.astype(jnp.bfloat16), "rep", scatter_dimension=1, tiled=True
        ).astype(jnp.float32),
        lax.psum_scatter(
            up_part.astype(jnp.bfloat16), "rep", scatter_dimension=1, tiled=True
        ).astype(jnp.float32),
        lax.psum_scatter(
            down_part.astype(jnp.bfloat16), "rep", scatter_dimension=1, tiled=True
        ).astype(jnp.float32),
    )
    route_grads = returned_grad[target].reshape(token_rows, chosen, width)
    d_tokens = jnp.sum(route_grads.astype(jnp.float32), axis=1).astype(jnp.bfloat16)
    d_probs = returned_prob[target].reshape(token_rows, chosen)
    return (d_tokens, d_probs, gate_grad, up_grad, down_grad)


def solution(mesh):
    placed = (
        P(("rep", "ep"), None),
        P(("rep", "ep"), None),
        P(("rep", "ep"), None),
        P(("rep", "ep"), None),
        P(("rep", "ep"), None),
        P(("rep", "ep"), None),
        P("ep", "rep", None),
        P("ep", "rep", None),
        P("ep", "rep", None),
    )
    return jax.shard_map(
        on_device,
        mesh=mesh,
        in_specs=placed,
        out_specs=(
            P(("rep", "ep"), None),
            P(("rep", "ep"), None),
            P("ep", "rep", None),
            P("ep", "rep", None),
            P("ep", "rep", None),
        ),
        check_vma=False,
    )
```

profile of v0, /device:TPU:6, one launch (start us, length us, event | category | flops | bytes accessed | tf_op | source)
XLA Modules:
  0.0 439.6 jit_solution(8914376971288652473)
XLA Ops:
  11.6 3.4 scatter_custom_fusion
  16.0 5.4 %gather_fusion = bf16[832]{0:T(1024)(128)(2,1)S(1)} fusion(bf16[769]{0:T(1024)(128)(2,1)S(1)} %pad_maximum_fusion, s32[1024]{0:T(1024)S(1)} %get-tuple-element.21), kind=kCustom, calls=%fused_computation | custom fusion | bytes 6656 | tf_op jit(solution)/shard_map/gather | solution.py:45
  22.2 12.1 %all-to-all-start = ((bf16[64,13,1]{1,2,0:T(2,128)(2,1)}), bf16[64,13,1]{1,2,0:T(2,128)(2,1)S(1)}, u32[]{:S(2)}, u32[]{:S(2)}) async-start(bf16[64,13,1]{1,2,0:T(2,128)(2,1)} %all_to_all.49), calls=%async_computation | async-start | bytes 65536 | tf_op jit(solution)/shard_map/all_to_all | solution.py:49
  34.3 4.9 %gather_fusion.1 = bf16[832,2048]{1,0:T(8,128)(2,1)} fusion(bf16[129,2048]{1,0:T(8,128)(2,1)S(1)} %concatenate.10, s32[1024]{0:T(1024)S(1)} %get-tuple-element.20), kind=kCustom, calls=%fused_computation.1 | custom fusion | bytes 6819072 | tf_op jit(solution)/shard_map/gather | solution.py:43
  39.3 4.9 %all_to_all.38 = bf16[64,13,2048]{2,1,0:T(8,128)(2,1)} reshape(bf16[832,2048]{1,0:T(8,128)(2,1)} %gather_fusion.1) | data formatting | bytes 6815744 | tf_op jit(solution)/shard_map/all_to_all | solution.py:47
  44.2 10.7 %all-to-all-start.1 = ((bf16[64,13,2048]{2,1,0:T(8,128)(2,1)}), bf16[64,13,2048]{2,1,0:T(8,128)(2,1)}, u32[]{:S(2)}, u32[]{:S(2)}) async-start(bf16[64,13,2048]{2,1,0:T(8,128)(2,1)} %all_to_all.38), calls=%async_computation.1 | async-start | bytes 8388608 | tf_op jit(solution)/shard_map/all_to_all | solution.py:47
  56.5 4.9 %gather_fusion.4 = bf16[832,2048]{1,0:T(8,128)(2,1)} fusion(bf16[129,2048]{1,0:T(8,128)(2,1)S(1)} %concatenate.11, s32[1024]{0:T(1024)S(1)} %get-tuple-element.20), kind=kCustom, calls=%fused_computation.4 | custom fusion | bytes 6819072 | tf_op jit(solution)/shard_map/gather | solution.py:44
  61.5 5.0 %all_to_all.46 = bf16[64,13,2048]{2,1,0:T(8,128)(2,1)} reshape(bf16[832,2048]{1,0:T(8,128)(2,1)} %gather_fusion.4) | data formatting | bytes 6815744 | tf_op jit(solution)/shard_map/all_to_all | solution.py:48
  66.4 84.2 %all-to-all-done.1 = bf16[64,13,2048]{2,1,0:T(8,128)(2,1)} async-done(((bf16[64,13,2048]{2,1,0:T(8,128)(2,1)}), bf16[64,13,2048]{2,1,0:T(8,128)(2,1)}, u32[]{:S(2)}, u32[]{:S(2)}) %all-to-all-start.1) | async-done | bytes 3407904 | tf_op jit(solution)/shard_map/all_to_all | solution.py:47
  150.7 6.1 %all-to-all-start.4 = ((bf16[64,13,2048]{2,1,0:T(8,128)(2,1)}), bf16[64,13,2048]{2,1,0:T(8,128)(2,1)}, u32[]{:S(2)}, u32[]{:S(2)}) async-start(bf16[64,13,2048]{2,1,0:T(8,128)(2,1)} %all_to_all.46), calls=%async_computation.4 | async-start | bytes 8388608 | tf_op jit(solution)/shard_map/all_to_all | solution.py:48
  158.0 3.5 all_to_all.40
  161.4 91.0 %all-to-all-done.4 = bf16[64,13,2048]{2,1,0:T(8,128)(2,1)} async-done(((bf16[64,13,2048]{2,1,0:T(8,128)(2,1)}), bf16[64,13,2048]{2,1,0:T(8,128)(2,1)}, u32[]{:S(2)}, u32[]{:S(2)}) %all-to-all-start.4) | async-done | bytes 3407904 | tf_op jit(solution)/shard_map/all_to_all | solution.py:48
  252.5 5.0 %all_to_all.48 = bf16[832,2048]{1,0:T(8,128)(2,1)} reshape(bf16[64,13,2048]{2,1,0:T(8,128)(2,1)} %all-to-all-done.4) | data formatting | bytes 6815744 | tf_op jit(solution)/shard_map/all_to_all | solution.py:48
  257.4 8.1 %multiply_reduce_fusion = (bf16[832]{0:T(1024)(128)(2,1)S(1)}, bf16[832,704]{0,1:T(8,128)(2,1)}, bf16[832,704]{0,1:T(8,128)(2,1)S(1)}) fusion(bf16[832,704]{0,1:T(8,128)(2,1)} %param.14, bf16[832,704]{0,1:T(8,128)(2,1)} %param.13, f32[832]{0:T(1024)S(1)} %reshape.102, bf16[832,2048]{1,0:T(8,128)(2,1)S(1)} %all_to_all.40, ...), kind=kOutput, calls=%fused_computation.34 | convolution fusion | flops 2411441408 | bytes 10982272 | tf_op jit(solution)/shard_map/dot_general | solution.py:14
  266.6 4.5 %fusion.4 = bf16[1,704,2048]{2,1,0:T(8,128)(2,1)} fusion(bf16[832,704]{0,1:T(8,128)(2,1)S(1)} %get-tuple-element.17, bf16[832,2048]{1,0:T(8,128)(2,1)S(1)} %copy-done), kind=kOutput, calls=%fused_computation.19 | convolution fusion | flops 2400583680 | bytes 7462912 | tf_op jit(solution)/shard_map/dot_general | solution.py:8
  271.2 7.1 %fusion.3 = bf16[1,704,2048]{2,1,0:T(8,128)(2,1)} fusion(bf16[832,704]{0,1:T(8,128)(2,1)} %get-tuple-element.16, bf16[832,2048]{1,0:T(8,128)(2,1)} %all_to_all.48), kind=kOutput, calls=%fused_computation.18 | convolution fusion | flops 2400583680 | bytes 7462912 | tf_op jit(solution)/shard_map/dot_general | solution.py:8
  279.0 6.1 %all-to-all-start.3 = ((bf16[64,13,1]{1,2,0:T(2,128)(2,1)}), bf16[64,13,1]{1,2,0:T(2,128)(2,1)S(1)}, u32[]{:S(2)}, u32[]{:S(2)}) async-start(bf16[64,13,1]{1,2,0:T(2,128)(2,1)} %convert_element_type.108), calls=%async_computation.3 | async-start | bytes 65536 | tf_op jit(solution)/shard_map/all_to_all | solution.py:80
  285.2 7.9 %fusion.7 = f32[832,2048]{1,0:T(8,128)} fusion(bf16[832,704]{0,1:T(8,128)(2,1)} %get-tuple-element.16, bf16[1,704,2048]{2,1,0:T(8,128)(2,1)} %all-gather.6.cloned.1.call-done), kind=kOutput, calls=%fused_computation.22 | convolution fusion | flops 2399141888 | bytes 10870784 | tf_op jit(solution)/shard_map/dot_general | solution.py:75
  293.1 8.9 %add_convert_fusion = bf16[832,2048]{1,0:T(8,128)(2,1)} fusion(f32[832,2048]{1,0:T(8,128)} %fusion.7, bf16[832,704]{0,1:T(8,128)(2,1)} %copy-done.3, bf16[1,704,2048]{2,1,0:T(8,128)(2,1)} %all-gather.8.cloned.1.call-done), kind=kOutput, calls=%fused_computation.7 | convolution fusion | flops 2402549760 | bytes 14278656 | tf_op jit(solution)/shard_map/dot_general | solution.py:76
  302.0 5.0 %all_to_all.41 = bf16[64,13,2048]{2,1,0:T(8,128)(2,1)} reshape(bf16[832,2048]{1,0:T(8,128)(2,1)} %add_convert_fusion) | data formatting | bytes 6815744 | tf_op jit(solution)/shard_map/all_to_all | solution.py:79
  307.0 10.4 %all-to-all-start.2 = ((bf16[64,13,2048]{2,1,0:T(8,128)(2,1)}), bf16[64,13,2048]{2,1,0:T(8,128)(2,1)}, u32[]{:S(2)}, u32[]{:S(2)}) async-start(bf16[64,13,2048]{2,1,0:T(8,128)(2,1)} %all_to_all.41), calls=%async_computation.2 | async-start | bytes 8388608 | tf_op jit(solution)/shard_map/all_to_all | solution.py:79
  317.7 6.8 %fusion.5 = bf16[1,704,2048]{2,1,0:T(8,128)(2,1)} fusion(bf16[832,2048]{1,0:T(8,128)(2,1)S(1)} %all_to_all.40, f32[832]{0:T(1024)S(1)} %reshape.102, bf16[832,704]{0,1:T(8,128)(2,1)} %param.14, bf16[832,704]{0,1:T(8,128)(2,1)} %param.13), kind=kOutput, calls=%fused_computation.20 | convolution fusion | flops 2410381312 | bytes 8637696 | tf_op jit(solution)/shard_map/dot_general | solution.py:8
  324.8 5.0 %gather_fusion.3 = bf16[768]{0:T(1024)(128)(2,1)S(1)} fusion(bf16[832]{0:T(1024)(128)(2,1)S(1)} %all_to_all.45, s32[1024]{0:T(1024)S(1)} %pad_clamp_fusion), kind=kCustom, calls=%fused_computation.3 | custom fusion | bytes 6144 | tf_op jit(solution)/shard_map/gather | solution.py:97
  330.7 2.4 convert_element_type.101
  333.0 12.6 %reduce-scatter.4.cloned.1.call-done = bf16[1,176,2048]{2,1,0:T(8,128)(2,1)} async-done(((bf16[1,704,2048]{2,1,0:T(8,128)(2,1)}), bf16[1,176,2048]{2,1,0:T(8,128)(2,1)}) %reduce-scatter.4.cloned.1.call-update) | async-done | bytes 720912 | tf_op jit(solution)/shard_map/reduce_scatter | solution.py:85
  345.6 2.4 convert_element_type.98
  348.0 38.5 %reduce-scatter.8.cloned.1.call-done = bf16[1,176,2048]{2,1,0:T(8,128)(2,1)} async-done(((bf16[1,704,2048]{2,1,0:T(8,128)(2,1)}), bf16[1,176,2048]{2,1,0:T(8,128)(2,1)}) %reduce-scatter.8.cloned.1.call-update) | async-done | bytes 720912 | tf_op jit(solution)/shard_map/reduce_scatter | solution.py:91
  388.8 24.3 %all-to-all-done.2 = bf16[64,13,2048]{2,1,0:T(8,128)(2,1)} async-done(((bf16[64,13,2048]{2,1,0:T(8,128)(2,1)}), bf16[64,13,2048]{2,1,0:T(8,128)(2,1)}, u32[]{:S(2)}, u32[]{:S(2)}) %all-to-all-start.2) | async-done | bytes 3407904 | tf_op jit(solution)/shard_map/all_to_all | solution.py:79
  413.1 3.4 all_to_all.43
  416.6 4.3 gather_fusion.2
  420.8 6.3 %reshape.100 = bf16[128,6,2048]{2,1,0:T(8,128)(2,1)} reshape(bf16[768,2048]{1,0:T(8,128)(2,1)} %gather_fusion.2) | data formatting | bytes 6291456 | tf_op jit(solution)/shard_map/reshape | solution.py:95
  427.1 5.7 %reduce_sum.34 = bf16[128,2048]{1,0:T(8,128)(2,1)} reduce(bf16[128,6,2048]{2,1,0:T(8,128)(2,1)} %reshape.100, bf16[]{:T(256)} %constant.12.clone.1), dimensions={1}, to_apply=%region_4.5 | reduce | flops 1310720 | bytes 3670018 | tf_op jit(solution)/shard_map/reduce_sum | solution.py:96
  (56 shorter events, 14.5 us)
Async XLA Ops:
  7.2 27.1 %copy-start.1 = (bf16[128,2048]{1,0:T(8,128)(2,1)S(1)}, bf16[128,2048]{1,0:T(8,128)(2,1)}, u32[]{:S(2)}) copy-start(bf16[128,2048]{1,0:T(8,128)(2,1)} %param.9) | copy-start | bytes 1572868
  22.2 22.1 %all-to-all-start = ((bf16[64,13,1]{1,2,0:T(2,128)(2,1)}), bf16[64,13,1]{1,2,0:T(2,128)(2,1)S(1)}, u32[]{:S(2)}, u32[]{:S(2)}) async-start(bf16[64,13,1]{1,2,0:T(2,128)(2,1)} %all_to_all.49), calls=%async_computation | async-start | bytes 65536 | tf_op jit(solution)/shard_map/all_to_all | solution.py:49
  44.2 12.2 %copy-start.2 = (bf16[128,2048]{1,0:T(8,128)(2,1)S(1)}, bf16[128,2048]{1,0:T(8,128)(2,1)}, u32[]{:S(2)}) copy-start(bf16[128,2048]{1,0:T(8,128)(2,1)} %param.10) | copy-start | bytes 1572868
  44.2 106.4 %all-to-all-start.1 = ((bf16[64,13,2048]{2,1,0:T(8,128)(2,1)}), bf16[64,13,2048]{2,1,0:T(8,128)(2,1)}, u32[]{:S(2)}, u32[]{:S(2)}) async-start(bf16[64,13,2048]{2,1,0:T(8,128)(2,1)} %all_to_all.38), calls=%async_computation.1 | async-start | bytes 8388608 | tf_op jit(solution)/shard_map/all_to_all | solution.py:47
  55.0 202.5 %all-gather.4.cloned.1.call-start = ((), (), s32[]{:S(2)}) async-start(), calls=%async_computation.8 | async-start | bytes 3604480 | tf_op jit(solution)/shard_map/all_gather | solution.py:54
  55.7 229.5 %all-gather.6.cloned.1.call-start = ((), (), s32[]{:S(2)}) async-start(), calls=%async_computation.9 | async-start | bytes 3604480 | tf_op jit(solution)/shard_map/all_gather | solution.py:52
  150.7 101.8 %all-to-all-start.4 = ((bf16[64,13,2048]{2,1,0:T(8,128)(2,1)}), bf16[64,13,2048]{2,1,0:T(8,128)(2,1)}, u32[]{:S(2)}, u32[]{:S(2)}) async-start(bf16[64,13,2048]{2,1,0:T(8,128)(2,1)} %all_to_all.46), calls=%async_computation.4 | async-start | bytes 8388608 | tf_op jit(solution)/shard_map/all_to_all | solution.py:48
  156.8 136.3 %all-gather.8.cloned.1.call-start = ((), (), s32[]{:S(2)}) async-start(), calls=%async_computation.10 | async-start | bytes 3604480 | tf_op jit(solution)/shard_map/all_gather | solution.py:53
  157.5 173.1 %reduce-scatter.6.cloned.1.call-start = ((), (), s32[]{:S(2)}) async-start(), calls=%async_computation.12 | async-start | bytes 3604480 | tf_op jit(solution)/shard_map/reduce_scatter | solution.py:88
  257.4 9.2 %copy-start = (bf16[832,2048]{1,0:T(8,128)(2,1)S(1)}, bf16[832,2048]{1,0:T(8,128)(2,1)}, u32[]{:S(2)}) copy-start(bf16[832,2048]{1,0:T(8,128)(2,1)} %all_to_all.48) | copy-start | bytes 10223620
  265.6 1.0 copy-start.3
  271.1 74.5 %reduce-scatter.4.cloned.1.call-start = ((), (), s32[]{:S(2)}) async-start(), calls=%async_computation.11 | async-start | bytes 3604480 | tf_op jit(solution)/shard_map/reduce_scatter | solution.py:85
  279.0 27.9 %all-to-all-start.3 = ((bf16[64,13,1]{1,2,0:T(2,128)(2,1)}), bf16[64,13,1]{1,2,0:T(2,128)(2,1)S(1)}, u32[]{:S(2)}, u32[]{:S(2)}) async-start(bf16[64,13,1]{1,2,0:T(2,128)(2,1)} %convert_element_type.108), calls=%async_computation.3 | async-start | bytes 65536 | tf_op jit(solution)/shard_map/all_to_all | solution.py:80
  307.0 106.1 %all-to-all-start.2 = ((bf16[64,13,2048]{2,1,0:T(8,128)(2,1)}), bf16[64,13,2048]{2,1,0:T(8,128)(2,1)}, u32[]{:S(2)}, u32[]{:S(2)}) async-start(bf16[64,13,2048]{2,1,0:T(8,128)(2,1)} %all_to_all.41), calls=%async_computation.2 | async-start | bytes 8388608 | tf_op jit(solution)/shard_map/all_to_all | solution.py:79
  317.4 69.1 %reduce-scatter.8.cloned.1.call-start = ((), (), s32[]{:S(2)}) async-start(), calls=%async_computation.13 | async-start | bytes 3604480 | tf_op jit(solution)/shard_map/reduce_scatter | solution.py:91
Sparse Core Ops, SparseCore 0:
  57.6 39.0 all-gather.3
  98.5 40.0 all-gather.5
  159.4 39.0 all-gather.7
  271.2 33.4 reduce-scatter.5
  307.2 38.4 reduce-scatter.3
  348.0 38.3 reduce-scatter.7
where the time goes:
time: 442 us; the launch traced here: 440 us
  waiting for transfers between devices  253 us (57%)
  local copies, waits for them, and re-layouts  67.4 us (15%)
  starting transfers between devices  46.2 us (10%)
  matrix products  43.3 us (10%)
  other arithmetic  15.7 us (4%)
  between operations  14.3 us (3%)
    all_to_all x1, waiting for transfers between devices, on_device(): lax.all_to_all(send_input, 'ep', split_axis=0, concat_axis=0, tiled=True)  91 us
    all_to_all x1, waiting for transfers between devices, on_device(): lax.all_to_all(send_grad, 'ep', split_axis=0, concat_axis=0, tiled=True)  84.2 us
    reduce_scatter x1, waiting for transfers between devices, on_device(): lax.psum_scatter(down_part.astype(jnp.bfloat16), 'rep', scatter_dimension...  38.5 us
    all_to_all x1, waiting for transfers between devices, on_device(): lax.all_to_all(input_grad, 'ep', split_axis=0, concat_axis=0, tiled=True)  24.3 us
    dot_general x3, matrix products, contract_rows(): lax.dot_general(left, right, (((0,), (0,)), ((), ())), preferred_element_...  18.4 us
    reduce_scatter x1, waiting for transfers between devices, on_device(): lax.psum_scatter(gate_part.astype(jnp.bfloat16), 'rep', scatter_dimension...  12.6 us
    all_to_all x1, starting transfers between devices, on_device(): lax.all_to_all(send_weight, 'ep', split_axis=0, concat_axis=0, tiled=True)  12.1 us
    all_to_all x1, starting transfers between devices, on_device(): lax.all_to_all(send_grad, 'ep', split_axis=0, concat_axis=0, tiled=True)  10.7 us
  transfers between devices with their start and end apart: 11, of which 5 were waited for; matrix products, arithmetic and copies ran while one was open for 15% of the time, Pallas kernels for 0%

commit v1 on v0

v1 whole, which is shorter than its diff:
```python
import jax
import jax.numpy as jnp
from jax import lax
from jax.experimental import pallas as pl
from jax.experimental.pallas import tpu as pltpu
from jax.sharding import PartitionSpec as P

NX, NY, NZ, NC = 4, 4, 8, 2
NG = NY * NC
CAP, TOP = 13, 6
T = 128
D, H = 2048, 704
HS = H // NX
NK = 4
CW = D // NK
GR = 128
GS = 112
S = NG * GR
HALF = D // 2
DOWN, GATE, UP = 0, 1, 2
MESH = pl.DeviceIdType.MESH
F32, BF16 = jnp.float32, jnp.bfloat16
Y_OFFSETS = [(dy, dc) for dy in range(NY) for dc in range(NC) if (dy, dc) != (0, 0)]


def nn(a, b):
    return jnp.dot(a, b, preferred_element_type=F32)


def nt(a, b):
    return lax.dot_general(a, b, (((1,), (1,)), ((), ())), preferred_element_type=F32)


def iota(shape, dim):
    return lax.broadcasted_iota(jnp.int32, shape, dim)


def div13(r):
    return (r * 79) >> 10


def body(
    d_out, saved, routes_t, probs_t, gpre, upre, dw, gw, uw,
    dtok, dprob, dg, gg, ug,
    wfull, zb, ys, slots, oh, oht, gp, up, aw, gbt, ubt, pt0, zrecv, xrel, xfin, stage, psum,
    meta_out, meta_in, ws, wr, ps, pr, dps, dpr,
    ag_s, ag_r, rs_s, rs_r, zs_s, zs_r, tz_s, tz_r, yd_s, yd_r, yr_s, yr_r,
    m_s, m_r, w_s, w_r, p_s, p_r, q_s, q_r, loc, out_sem,
):
    x = lax.axis_index("rep")
    ep = lax.axis_index("ep")
    core = lax.rem(ep, NC)
    z = lax.rem(ep // NC, NZ)
    y = ep // (NC * NZ)
    me_g = y * NC + core

    def at_x(d):
        return lax.rem(x + d + NX, NX)

    def at_z(d):
        return lax.rem(z + d + NZ, NZ)

    def dev_x(d):
        return (at_x(d), ep)

    def dev_z(d):
        return (x, (y * NZ + at_z(d)) * NC + core)

    def dev_y(i):
        dy, dc = Y_OFFSETS[i]
        y2, c2 = lax.rem(y + dy, NY), lax.rem(core + dc, NC)
        return y2 * NC + c2, (x, (y2 * NZ + z) * NC + c2)

    def remote(src, dst, send, recv, device):
        return pltpu.make_async_remote_copy(
            src_ref=src, dst_ref=dst, send_sem=send, recv_sem=recv,
            device_id=device, device_id_type=MESH,
        )

    barrier = pltpu.get_barrier_semaphore()
    peers = [dev_x(1), dev_x(-1)] + [dev_z(d) for d in range(1, NZ)]
    peers += [dev_y(i)[1] for i in range(len(Y_OFFSETS))]
    for device in peers:
        pl.semaphore_signal(barrier, inc=1, device_id=device, device_id_type=MESH)

    own = []
    for a, ref in enumerate((d_out, saved)):
        for k in range(NK):
            own.append(
                pltpu.make_async_copy(
                    ref.at[:, pl.ds(k * CW, CW)], zb.at[a, k, z], loc.at[a * NK + k]
                )
            )
    for cp in own:
        cp.start()
    shards = (dw, gw, uw)
    own_w = [pltpu.make_async_copy(shards[a], wfull.at[a, x], loc.at[2 * NK + a]) for a in range(3)]
    for cp in own_w:
        cp.start()
    pl.semaphore_wait(barrier, len(peers))

    def ag_copy(a, i):
        if i == 0:
            return remote(shards[a], wfull.at[a, x], ag_s.at[a, 0], ag_r.at[a, 0], dev_x(1))
        if i == 1:
            return remote(shards[a], wfull.at[a, x], ag_s.at[a, 1], ag_r.at[a, 1], dev_x(-1))
        if i == 2:
            ref = wfull.at[a, at_x(-1), :, pl.ds(0, HALF)]
            return remote(ref, ref, ag_s.at[a, 2], ag_r.at[a, 2], dev_x(1))
        ref = wfull.at[a, at_x(1), :, pl.ds(HALF, HALF)]
        return remote(ref, ref, ag_s.at[a, 3], ag_r.at[a, 3], dev_x(-1))

    def ag_start(a):
        ag_copy(a, 0).start()
        ag_copy(a, 1).start()

    def ag_relay(a):
        ag_copy(a, 0).wait_recv()
        ag_copy(a, 2).start()
        ag_copy(a, 1).wait_recv()
        ag_copy(a, 3).start()

    def ag_finish(a):
        ag_copy(a, 2).wait_recv()
        ag_copy(a, 3).wait_recv()
        own_w[a].wait()
        for i in range(4):
            ag_copy(a, i).wait_send()

    def hops(k):
        return (4, 3) if k % 2 == 0 else (3, 4)

    def zag_copy(a, k, way, s):
        sign = 1 if way == 0 else -1
        i = s if way == 0 else hops(k)[0] + s
        ref = zb.at[a, k, at_z(-sign * s)]
        return remote(ref, ref, zs_s.at[a, k, i], zs_r.at[a, k, i], dev_z(sign))

    def zag_step(n, s):
        a, k = n // NK, n % NK
        if s == 0:
            own[n].wait()
        for way in range(2):
            if 1 <= s <= hops(k)[way]:
                zag_copy(a, k, way, s - 1).wait_recv()
            if s < hops(k)[way]:
                zag_copy(a, k, way, s).start()

    def zag_sent(n):
        a, k = n // NK, n % NK
        for way in range(2):
            for s in range(hops(k)[way]):
                zag_copy(a, k, way, s).wait_send()

    def yd_copy(a, k, i):
        g, device = dev_y(i)
        return remote(
            ys.at[k % 2, g, pl.ds(0, GS)], slots.at[a, k, me_g, pl.ds(0, GS)],
            yd_s.at[a, k, i], yd_r.at[a, k, i], device,
        )

    def dispatch(n):
        a, k = n // NK, n % NK
        zag_sent(n)
        if n >= 2:
            for i in range(7):
                yd_copy((n - 2) // NK, (n - 2) % NK, i).wait_send()
        rows = nn(oh[...].reshape(S, NZ * T), zb[a, k].reshape(NZ * T, CW))
        ys[k % 2] = rows.astype(BF16).reshape(NG, GR, CW)
        for i in range(7):
            yd_copy(a, k, i).start()
        slots[a, k, me_g] = ys[k % 2, me_g]

    def m_copy(d):
        return remote(meta_out.at[at_z(d)], meta_in.at[z], m_s.at[d - 1], m_r.at[d - 1], dev_z(d))

    def w_copy(i):
        g, device = dev_y(i)
        return remote(ws.at[g], wr.at[me_g], w_s.at[i], w_r.at[i], device)

    def p_copy(i):
        g, device = dev_y(i)
        return remote(ps.at[g], pr.at[me_g], p_s.at[i], p_r.at[i], device)

    def q_copy(d):
        return remote(dps.at[at_z(d)], dpr.at[z], q_s.at[d - 1], q_r.at[d - 1], dev_z(d))

    def expert_of_row():
        q = iota((NZ * NG, T), 0)
        return (((q >> 1) & 3) * NZ + (q >> 3)) * NC + (q & 1)

    def send_meta():
        ids = expert_of_row()
        hit_sum = jnp.zeros((NZ * NG, T), F32)
        prob_sum = jnp.zeros((NZ * NG, T), F32)
        for k in range(TOP):
            hit = ids == routes_t[k : k + 1, :]
            hit_sum = hit_sum + jnp.where(hit, 1.0, 0.0)
            prob_sum = prob_sum + jnp.where(hit, probs_t[k : k + 1, :].astype(F32), 0.0)
        before = jnp.where(iota((T, T), 0) < iota((T, T), 1), 1.0, 0.0).astype(BF16)
        rank = hit_sum * (nn(hit_sum.astype(BF16), before) + 1.0)
        for d in range(NZ):
            part = slice(d * NG, (d + 1) * NG)
            meta_out[d] = jnp.concatenate([rank[part], prob_sum[part]], axis=0).astype(BF16)
        for d in range(1, NZ):
            m_copy(d).start()
        meta_in[z] = meta_out[z]

    def permute_slots():
        n = iota((1, S), 1)
        g, r = n >> 7, n & 127
        zr = div13(r)
        slot = (((g >> 1) * NZ + zr) * NC + (g & 1)) * CAP + (r - zr * CAP)
        slot = jnp.where(r < NZ * CAP, slot, -1)
        perm = jnp.where(iota((NG * NZ * CAP, S), 0) == slot, 1.0, 0.0).astype(BF16)
        for j in range(NX):
            gp[j] = nn(gpre[pl.ds(j * HS, HS), :], perm).astype(BF16)
            up[j] = nn(upre[pl.ds(j * HS, HS), :], perm).astype(BF16)

    def build_tables():
        for d in range(1, NZ):
            m_copy(d).wait()
        table = jnp.concatenate([meta_in[d].astype(F32) for d in range(NZ)], axis=1)
        r = iota((GR, NZ * T), 0)
        zr = div13(r)
        key = jnp.where(
            (zr == (iota((GR, NZ * T), 1) >> 7)) & (r < NZ * CAP), r - zr * CAP + 1, -1
        ).astype(F32)
        for g in range(NG):
            oh[g] = jnp.where(table[g : g + 1, :] == key, 1.0, 0.0).astype(BF16)
        table16 = table.astype(BF16)
        for g in range(NG):
            rows = nt(table16, oh[g])
            ws[g] = jnp.broadcast_to(rows[NG + g : NG + g + 1, :], (16, GR)).astype(BF16)
        for i in range(7):
            w_copy(i).start()
        wr[me_g] = ws[me_g]

    def transpose_tables():
        for g in range(NG):
            oht[:, pl.ds(g * GR, GR)] = oh[g].T

    def tile_down(i):
        j = at_x(2 + i)
        back = jnp.zeros((HS, S), F32)
        for k in range(NK):
            back = back + nt(wfull[DOWN, j, :, pl.ds(k * CW, CW)], slots[0, k].reshape(S, CW))
        weight = jnp.concatenate([wr[g][0:1, :].astype(F32) for g in range(NG)], axis=1)
        gate_val, up_val = gp[j].astype(F32), up[j].astype(F32)
        logistic = 1.0 / (1.0 + jnp.exp(-gate_val))
        silu = gate_val * logistic
        act = (silu * up_val).astype(BF16).astype(F32)
        total = jnp.sum(back * act, axis=0, keepdims=True)
        if i == 0:
            psum[0:1, :] = total
        else:
            psum[0:1, :] = psum[0:1, :] + total
        scaled = weight * back
        aw[j] = (weight * act).astype(BF16)
        gp[j] = (scaled * up_val * logistic * (1.0 + gate_val * (1.0 - logistic))).astype(BF16)
        up[j] = (scaled * silu).astype(BF16)
        for k in range(NK):
            pt0[j, :, pl.ds(k * CW, CW)] = nn(aw[j], slots[0, k].reshape(S, CW)).astype(BF16)

    def tile_part(j, left, dst):
        for k in range(NK):
            dst[j, :, pl.ds(k * CW, CW)] = nn(left[j], slots[1, k].reshape(S, CW)).astype(BF16)

    parts = (pt0, wfull.at[DOWN], wfull.at[GATE])
    low, high = pl.ds(0, HALF), pl.ds(HALF, HALF)

    def rs_copy(a, i):
        p = parts[a]
        if i == 0:
            src, dst, device = p.at[at_x(2), :, low], xrel.at[a, 0], dev_x(1)
        elif i == 1:
            src, dst, device = p.at[at_x(2), :, high], xrel.at[a, 1], dev_x(-1)
        elif i == 2:
            src, dst, device = p.at[at_x(1), :, high], xfin.at[a, 0, :, high], dev_x(1)
        elif i == 3:
            src, dst, device = p.at[at_x(-1), :, low], xfin.at[a, 1, :, low], dev_x(-1)
        elif i == 4:
            src, dst, device = p.at[at_x(1), :, low], xfin.at[a, 0, :, low], dev_x(1)
        else:
            src, dst, device = p.at[at_x(-1), :, high], xfin.at[a, 1, :, high], dev_x(-1)
        return remote(src, dst, rs_s.at[a, i], rs_r.at[a, i], device)

    def rs_start(a):
        for i in range(4):
            rs_copy(a, i).start()

    def rs_relay(a):
        p = parts[a]
        rs_copy(a, 0).wait_recv()
        right = at_x(1)
        p[right, :, low] = (p[right, :, low].astype(F32) + xrel[a, 0].astype(F32)).astype(BF16)
        rs_copy(a, 4).start()
        rs_copy(a, 1).wait_recv()
        left = at_x(-1)
        p[left, :, high] = (p[left, :, high].astype(F32) + xrel[a, 1].astype(F32)).astype(BF16)
        rs_copy(a, 5).start()

    def out_copy(a):
        return pltpu.make_async_copy(stage, (dg, gg, ug)[a], out_sem)

    def rs_finish(a):
        for i in range(2, 6):
            rs_copy(a, i).wait_recv()
        if a != DOWN:
            out_copy(a - 1).wait()
        stage[...] = parts[a][x].astype(F32) + xfin[a, 0].astype(F32) + xfin[a, 1].astype(F32)
        out_copy(a).start()
        for i in range(6):
            rs_copy(a, i).wait_send()

    def yr_copy(k, i):
        g, device = dev_y(i)
        return remote(
            ys.at[k % 2, g, pl.ds(0, GS)], zb.at[0, k, me_g, pl.ds(0, GS)],
            yr_s.at[k, i], yr_r.at[k, i], device,
        )

    def give_back(k):
        cols = pl.ds(k * CW, CW)
        if k >= 2:
            for i in range(7):
                yr_copy(k - 2, i).wait_send()
        else:
            for i in range(7):
                yd_copy(1, k + 2, i).wait_send()
        rows = nn(gbt[...], wfull[GATE, :, :, cols].reshape(H, CW))
        rows = rows + nn(ubt[...], wfull[UP, :, :, cols].reshape(H, CW))
        ys[k % 2] = rows.astype(BF16).reshape(NG, GR, CW)
        for i in range(7):
            yr_copy(k, i).start()
        zb[0, k, me_g] = ys[k % 2, me_g]

    def tz_copy(k, way, s):
        sign = 1 if way == 0 else -1
        count = hops(k)[way]
        i = s if way == 0 else hops(k)[0] + s
        return remote(
            zb.at[1, k, at_z(sign * (count - s))], zrecv.at[k, i],
            tz_s.at[k, i], tz_r.at[k, i], dev_z(sign),
        )

    def combine(k):
        for i in range(7):
            yr_copy(k, i).wait_recv()
        total = nn(oht[...], zb[0, k].reshape(S, CW))
        zb[1, k] = total.astype(BF16).reshape(NZ, T, CW)

    def tz_step(k, s):
        if s == 0:
            combine(k)
        for way in range(2):
            sign, count = (1 if way == 0 else -1), hops(k)[way]
            base = 0 if way == 0 else hops(k)[0]
            if 1 <= s <= count:
                tz_copy(k, way, s - 1).wait_recv()
            if s < count:
                if s >= 1:
                    to = at_z(sign * (count - s))
                    zb[1, k, to] = (
                        zb[1, k, to].astype(F32) + zrecv[k, base + s - 1].astype(F32)
                    ).astype(BF16)
                tz_copy(k, way, s).start()
        if s == 4:
            first, second = hops(k)
            total = zb[1, k, z].astype(F32) + zrecv[k, first - 1].astype(F32)
            total = total + zrecv[k, first + second - 1].astype(F32)
            dtok[:, pl.ds(k * CW, CW)] = total.astype(BF16)

    send_meta()
    ag_start(0)
    zag_step(0, 0)
    ag_start(1)
    zag_step(1, 0)
    for a in range(2):
        for k in range(NK):
            slots[a, k, :, pl.ds(GS, GR - GS), :] = jnp.zeros((NG, GR - GS, CW), BF16)

    for slot in range(1, 2 * NK + 4):
        for s in range(4, -1, -1):
            n = slot - s
            if 0 <= n < 2 * NK and (n, s) not in ((0, 0), (1, 0)):
                zag_step(n, s)
        if slot == 1:
            build_tables()
        if slot == 2:
            permute_slots()
            ag_relay(0)
            ag_start(2)
        if slot == 3:
            transpose_tables()
        if slot >= 4:
            dispatch(slot - 4)
        if slot == 5:
            ag_relay(1)
        if slot == 7:
            ag_relay(2)
            ag_finish(0)
        if slot == 8:
            for i in range(7):
                w_copy(i).wait()
        if slot == 9:
            for k in range(NK):
                for i in range(7):
                    yd_copy(0, k, i).wait_recv()
            tile_down(0)
        if slot == 10:
            tile_down(1)
            tile_down(2)
    tile_down(3)
    rs_start(DOWN)

    for g in range(NG):
        cols = pl.ds(g * GR, GR)
        ps[g] = jnp.broadcast_to(psum[0:1, cols], (16, GR)).astype(BF16)
        gbt[cols, :] = gp[:, :, cols].reshape(H, GR).T
        ubt[cols, :] = up[:, :, cols].reshape(H, GR).T
    for i in range(7):
        p_copy(i).start()
    pr[me_g] = ps[me_g]
    ag_finish(1)
    ag_finish(2)
    for k in range(NK):
        give_back(k)
    for k in range(NK):
        for i in range(7):
            yd_copy(1, k, i).wait_recv()
    for i in range(NX):
        tile_part(at_x(2 + i), gp, parts[GATE])
    rs_start(GATE)
    rs_relay(DOWN)
    for i in range(NX):
        tile_part(at_x(2 + i), up, parts[UP])
    rs_start(UP)

    for i in range(7):
        p_copy(i).wait()
    dense = []
    for g in range(NG):
        dense.append(nn(pr[g], oh[g])[0:1, :])
    dense = jnp.concatenate(dense, axis=0)
    for d in range(NZ):
        part = dense[:, d * T : (d + 1) * T]
        dps[d] = jnp.concatenate([part, jnp.zeros((16 - NG, T), F32)], axis=0).astype(BF16)
    for d in range(1, NZ):
        q_copy(d).start()
    dpr[z] = dps[z]

    for slot in range(NK + 4):
        for s in range(4, -1, -1):
            k = slot - s
            if 0 <= k < NK:
                tz_step(k, s)
        if slot == 1:
            rs_finish(DOWN)
        if slot == 3:
            rs_relay(GATE)
            for d in range(1, NZ):
                q_copy(d).wait()
            ids = expert_of_row()
            table = jnp.concatenate([dpr[d][0:NG, :].astype(F32) for d in range(NZ)], axis=0)
            rows = []
            for k in range(TOP):
                hit = ids == routes_t[k : k + 1, :]
                rows.append(jnp.sum(jnp.where(hit, table, 0.0), axis=0, keepdims=True))
            dprob[...] = jnp.concatenate(rows, axis=0).astype(BF16)
        if slot == 5:
            rs_relay(UP)
        if slot == 6:
            rs_finish(GATE)
    rs_finish(UP)
    for k in range(NK):
        for way in range(2):
            for s in range(hops(k)[way]):
                tz_copy(k, way, s).wait_send()
    for k in (NK - 2, NK - 1):
        for i in range(7):
            yr_copy(k, i).wait_send()
    out_copy(UP).wait()


def on_device(
    d_out, saved_input, routes, probs, gate_pre, up_pre, gate_weight, up_weight, down_weight
):
    any_space = pl.BlockSpec(memory_space=pl.ANY)
    vmem = pl.BlockSpec(memory_space=pltpu.VMEM)
    dma = pltpu.SemaphoreType.DMA
    weight_grad = jax.ShapeDtypeStruct((HS, D), F32)
    d_tokens, d_probs, down_grad, gate_grad, up_grad = pl.pallas_call(
        body,
        out_shape=(
            jax.ShapeDtypeStruct((T, D), BF16),
            jax.ShapeDtypeStruct((TOP, T), BF16),
            weight_grad,
            weight_grad,
            weight_grad,
        ),
        in_specs=[any_space] * 2 + [vmem] * 4 + [any_space] * 3,
        out_specs=(vmem, vmem, any_space, any_space, any_space),
        scratch_shapes=[
            pltpu.VMEM((3, NX, HS, D), BF16),
            pltpu.VMEM((2, NK, NZ, T, CW), BF16),
            pltpu.VMEM((2, NG, GR, CW), BF16),
            pltpu.VMEM((2, NK, NG, GR, CW), BF16),
            pltpu.VMEM((NG, GR, NZ * T), BF16),
            pltpu.VMEM((NZ * T, S), BF16),
            pltpu.VMEM((NX, HS, S), BF16),
            pltpu.VMEM((NX, HS, S), BF16),
            pltpu.VMEM((NX, HS, S), BF16),
            pltpu.VMEM((S, H), BF16),
            pltpu.VMEM((S, H), BF16),
            pltpu.VMEM((NX, HS, D), BF16),
            pltpu.VMEM((NK, 7, T, CW), BF16),
            pltpu.VMEM((3, 2, HS, HALF), BF16),
            pltpu.VMEM((3, 2, HS, D), BF16),
            pltpu.VMEM((HS, D), F32),
            pltpu.VMEM((8, S), F32),
        ]
        + [pltpu.VMEM((8, 16, T), BF16)] * 8
        + [dma((3, 4)), dma((3, 4)), dma((3, 6)), dma((3, 6))]
        + [dma((2, NK, 7)), dma((2, NK, 7)), dma((NK, 7)), dma((NK, 7))]
        + [dma((2, NK, 7)), dma((2, NK, 7)), dma((NK, 7)), dma((NK, 7))]
        + [dma((7,))] * 8
        + [dma((2 * NK + 3,)), dma],
        compiler_params=pltpu.CompilerParams(
            collective_id=0, has_side_effects=True, vmem_limit_bytes=62 * 2**20
        ),
        cost_estimate=pl.CostEstimate(
            flops=16 * 10**9, bytes_accessed=20 * 10**6, transcendentals=10**6
        ),
    )(
        d_out, saved_input, routes.T, probs.T, gate_pre.T, up_pre.T,
        down_weight[0], gate_weight[0], up_weight[0],
    )
    return d_tokens, d_probs.T, gate_grad[None], up_grad[None], down_grad[None]


def solution(mesh):
    token = P(("rep", "ep"), None)
    weight = P("ep", "rep", None)
    return jax.shard_map(
        on_device,
        mesh=mesh,
        in_specs=(token,) * 6 + (weight,) * 3,
        out_specs=(token, token, weight, weight, weight),
        check_vma=False,
    )
```

time: 442 us -> 227 us (0.51)
  waiting for transfers between devices: 253 us -> 0 us
  Pallas kernels: 0 us -> 217 us
  local copies, waits for them, and re-layouts: 67.4 us -> 8.84 us
  starting transfers between devices: 46.2 us -> 0 us
  matrix products: 43.3 us -> 0 us
  other arithmetic: 15.7 us -> 0 us
  between operations: 14.3 us -> 0.65 us
    pallas_call x0 -> x1, Pallas kernels: none -> 217 us  [on_device(): pl.pallas_call(body, out_shape=(jax.ShapeDtypeStruct((T, D), BF16), jax.S...]
    all_to_all x5 -> x0, waiting for transfers between devices: 200 us -> none  [the longest x1 91 us: on_device(): lax.all_to_all(send_input, 'ep', split_axis=0, concat_axis=0, tiled=True)]
    reduce_scatter x3 -> x0, waiting for transfers between devices: 51.1 us -> none  [the longest x1 38.5 us: on_device(): lax.psum_scatter(down_part.astype(jnp.bfloat16), 'rep', scatter_dimension...]
    all_to_all x5 -> x0, starting transfers between devices: 45.5 us -> none  [the longest x1 12.1 us: on_device(): lax.all_to_all(send_weight, 'ep', split_axis=0, concat_axis=0, tiled=True)]
    dot_general x6 -> x0, matrix products: 43.3 us -> none  [the longest x3 18.4 us: contract_rows(): lax.dot_general(left, right, (((0,), (0,)), ((), ())), preferred_element_...]
    all_to_all x8 -> x0, local copies, waits for them, and re-layouts: 27.6 us -> none  [the longest x2 9.93 us: on_device(): lax.all_to_all(send_input, 'ep', split_axis=0, concat_axis=0, tiled=True)]
    gather x5 -> x0, local copies, waits for them, and re-layouts: 24.6 us -> none  [the longest x1 5.43 us: on_device(): send_weight = prob_ext[slot_owner]]
    convert_element_type x5 -> x0, other arithmetic: 7.22 us -> none  [the longest x3 7.11 us: on_device(): gate_grad, up_grad, down_grad = (lax.psum_scatter(gate_part.astype(jnp.bf...]
  transfers between devices with their start and end apart: 11 -> 0, of which waited for: 5 -> 0; matrix products, arithmetic and copies ran while one was open for 15% -> 0% of each run, Pallas kernels for 0% -> 0%
where the time goes in v1:
time: 227 us; the launch traced here: 226 us
  Pallas kernels  217 us (96%)
  local copies, waits for them, and re-layouts  8.84 us (4%)
    pallas_call x1, Pallas kernels, on_device(): pl.pallas_call(body, out_shape=(jax.ShapeDtypeStruct((T, D), BF16), jax.S...  217 us
    unnamed x9, local copies, waits for them, and re-layouts  8.84 us

profile of v1, /device:TPU:6, one launch (start us, length us, event | category | flops | bytes accessed | tf_op | source)
XLA Modules:
  0.0 226.1 jit_solution(16438535678737046454)
XLA Ops:
  0.6 216.7 %shard_map.128 = (bf16[128,2048]{1,0:T(8,128)(2,1)}, bf16[6,128]{1,0:T(8,128)(2,1)}, f32[176,2048]{1,0:T(8,128)}, f32[176,2048]{1,0:T(8,128)}, f32[176,2048]{1,0:T(8,128)}) custom-call(bf16[128,2048]{1,0:T(8,128)(2,1)} %d_out.1, bf16[128,2048]{1,0:T(8,128)(2,1)} %saved.1, s32[6,128]{1,0:T(8,128)} %bitcast.20, bf16[6,128]{1,0:T(8,128)(2,1)} %bitcast.21, ...), custom_call_target="tpu_custom_call" | custom-call | flops 16000000000 | bytes 20000000 | tf_op jit(solution)/shard_map/pallas_call | solution.py:493
  217.3 1.9 copy.19
  219.2 1.2 copy.20
  220.4 0.0 copy-start.1
  220.4 2.7 %copy.21 = f32[1,176,2048]{2,1,0:T(8,128)} copy(f32[1,176,2048]{2,1,0:T(8,128)} %bitcast.13) | data formatting | bytes 2883584
  223.2 0.0 copy-done.1
  223.2 0.0 copy-start
  223.2 1.1 copy.22
  224.3 0.8 copy-done
  225.0 1.1 copy.23
Async XLA Ops:
  220.4 2.7 %copy-start.1 = (f32[176,2048]{1,0:T(8,128)S(1)}, f32[176,2048]{1,0:T(8,128)}, u32[]{:S(2)}) copy-start(f32[176,2048]{1,0:T(8,128)} %get-tuple-element.13) | copy-start | bytes 4325380
  223.2 1.9 copy-start

commit v2 on v1

v2 whole, which is shorter than its diff:
```python
import jax
import jax.numpy as jnp
from jax import lax
from jax.experimental import pallas as pl
from jax.experimental.pallas import tpu as pltpu
from jax.sharding import PartitionSpec as P

NX, NY, NZ, NC = 4, 4, 8, 2
NG = NY * NC
CAP, TOP = 13, 6
T = 128
D, H = 2048, 704
HS = H // NX
NK = 4
CW = D // NK
THERE = [(0, 0, 256), (0, 256, 256), (0, 512, 512), (0, 1024, 512), (0, 1536, 512)]
THERE += [(1, 0, 512), (1, 512, 512), (1, 1024, 512), (1, 1536, 512)]
BACK = [(0, 512), (512, 512), (1024, 512), (1536, 256), (1792, 256)]
NT, NB, NYS = len(THERE), len(BACK), 4
ORDER = [0, 1, 2, 3, 4, 5, 6, NT, NT + 1, NT + 2, 7, NT + 3, 8, NT + 4]
TURN = {chunk: place for place, chunk in enumerate(ORDER)}
GR = 128
GS = 112
S = NG * GR
HALF = D // 2
DOWN, GATE, UP = 0, 1, 2
MESH = pl.DeviceIdType.MESH
F32, BF16 = jnp.float32, jnp.bfloat16
Y_OFFSETS = [(dy, dc) for dy in range(NY) for dc in range(NC) if (dy, dc) != (0, 0)]


def nn(a, b):
    return jnp.dot(a, b, preferred_element_type=F32)


def nt(a, b):
    return lax.dot_general(a, b, (((1,), (1,)), ((), ())), preferred_element_type=F32)


def iota(shape, dim):
    return lax.broadcasted_iota(jnp.int32, shape, dim)


def div13(r):
    return (r * 79) >> 10


def body(
    d_out, saved, routes_t, probs_t, gpre, upre, dw, gw, uw,
    dtok, dprob, dg, gg, ug,
    wfull, zb, ys, slots, oh, oht, gp, up, aw, gbt, ubt, pt0, pt2, zrecv, xrel, xfin, stage, psum,
    meta_out, meta_in, ws, wr, ps, pr, dps, dpr,
    ag_s, ag_r, rs_s, rs_r, zs_s, zs_r, tz_s, tz_r, yd_s, yd_r, yr_s, yr_r,
    m_s, m_r, w_s, w_r, p_s, p_r, q_s, q_r, loc, out_sem,
):
    x = lax.axis_index("rep")
    ep = lax.axis_index("ep")
    core = lax.rem(ep, NC)
    z = lax.rem(ep // NC, NZ)
    y = ep // (NC * NZ)
    me_g = y * NC + core

    def at_x(d):
        return lax.rem(x + d + NX, NX)

    def at_z(d):
        return lax.rem(z + d + NZ, NZ)

    def dev_x(d):
        return (at_x(d), ep)

    def dev_z(d):
        return (x, (y * NZ + at_z(d)) * NC + core)

    def dev_y(i):
        dy, dc = Y_OFFSETS[i]
        y2, c2 = lax.rem(y + dy, NY), lax.rem(core + dc, NC)
        return y2 * NC + c2, (x, (y2 * NZ + z) * NC + c2)

    def remote(src, dst, send, recv, device):
        return pltpu.make_async_remote_copy(
            src_ref=src, dst_ref=dst, send_sem=send, recv_sem=recv,
            device_id=device, device_id_type=MESH,
        )

    barrier = pltpu.get_barrier_semaphore()
    peers = [dev_x(1), dev_x(-1)] + [dev_z(d) for d in range(1, NZ)]
    peers += [dev_y(i)[1] for i in range(len(Y_OFFSETS))]
    for device in peers:
        pl.semaphore_signal(barrier, inc=1, device_id=device, device_id_type=MESH)

    own = []
    for n, (a, col, width) in enumerate(THERE):
        cols = pl.ds(col, width)
        ref = (d_out, saved)[a]
        own.append(pltpu.make_async_copy(ref.at[:, cols], zb.at[a, z, :, cols], loc.at[n]))
    for cp in own:
        cp.start()
    shards = (dw, gw, uw)
    own_w = [pltpu.make_async_copy(shards[a], wfull.at[a, x], loc.at[NT + a]) for a in range(3)]
    for cp in own_w:
        cp.start()
    pl.semaphore_wait(barrier, len(peers))

    def ag_copy(a, i):
        if i == 0:
            return remote(shards[a], wfull.at[a, x], ag_s.at[a, 0], ag_r.at[a, 0], dev_x(1))
        if i == 1:
            return remote(shards[a], wfull.at[a, x], ag_s.at[a, 1], ag_r.at[a, 1], dev_x(-1))
        if i == 2:
            ref = wfull.at[a, at_x(-1), :, pl.ds(0, HALF)]
            return remote(ref, ref, ag_s.at[a, 2], ag_r.at[a, 2], dev_x(1))
        ref = wfull.at[a, at_x(1), :, pl.ds(HALF, HALF)]
        return remote(ref, ref, ag_s.at[a, 3], ag_r.at[a, 3], dev_x(-1))

    def ag_start(a):
        ag_copy(a, 0).start()
        ag_copy(a, 1).start()

    def ag_relay(a):
        ag_copy(a, 0).wait_recv()
        ag_copy(a, 2).start()
        ag_copy(a, 1).wait_recv()
        ag_copy(a, 3).start()

    def ag_finish(a):
        ag_copy(a, 2).wait_recv()
        ag_copy(a, 3).wait_recv()
        own_w[a].wait()
        for i in range(4):
            ag_copy(a, i).wait_send()

    def hops(k):
        return (4, 3) if k % 2 == 0 else (3, 4)

    def zag_copy(n, way, s):
        a, col, width = THERE[n]
        sign = 1 if way == 0 else -1
        i = s if way == 0 else hops(n)[0] + s
        ref = zb.at[a, at_z(-sign * s), :, pl.ds(col, width)]
        return remote(ref, ref, zs_s.at[n, i], zs_r.at[n, i], dev_z(sign))

    def zag_step(n, s):
        if s == 0:
            own[n].wait()
        for way in range(2):
            if 1 <= s <= hops(n)[way]:
                zag_copy(n, way, s - 1).wait_recv()
            if s < hops(n)[way]:
                zag_copy(n, way, s).start()

    def yd_copy(n, i):
        a, col, width = THERE[n]
        g, device = dev_y(i)
        return remote(
            ys.at[TURN[n] % NYS, g, pl.ds(0, GS), pl.ds(0, width)],
            slots.at[a, me_g, pl.ds(0, GS), pl.ds(col, width)],
            yd_s.at[n, i], yd_r.at[n, i], device,
        )

    def sent(chunk):
        for i in range(7):
            (yd_copy(chunk, i) if chunk < NT else yr_copy(chunk - NT, i)).wait_send()

    def free_buffer(chunk):
        if TURN[chunk] >= NYS:
            sent(ORDER[TURN[chunk] - NYS])

    def dispatch(n):
        a, col, width = THERE[n]
        for way in range(2):
            for s in range(hops(n)[way]):
                zag_copy(n, way, s).wait_send()
        free_buffer(n)
        rows = nn(oh[...].reshape(S, NZ * T), zb[a, :, :, pl.ds(col, width)].reshape(NZ * T, width))
        ys[TURN[n] % NYS, :, :, pl.ds(0, width)] = rows.astype(BF16).reshape(NG, GR, width)
        for i in range(7):
            yd_copy(n, i).start()
        slots[a, me_g, :, pl.ds(col, width)] = ys[TURN[n] % NYS, me_g, :, pl.ds(0, width)]

    def arrived(n):
        for i in range(7):
            yd_copy(n, i).wait_recv()

    def m_copy(d):
        return remote(meta_out.at[at_z(d)], meta_in.at[z], m_s.at[d - 1], m_r.at[d - 1], dev_z(d))

    def w_copy(i):
        g, device = dev_y(i)
        return remote(ws.at[g], wr.at[me_g], w_s.at[i], w_r.at[i], device)

    def p_copy(i):
        g, device = dev_y(i)
        return remote(ps.at[g], pr.at[me_g], p_s.at[i], p_r.at[i], device)

    def q_copy(d):
        return remote(dps.at[at_z(d)], dpr.at[z], q_s.at[d - 1], q_r.at[d - 1], dev_z(d))

    def expert_of_row():
        q = iota((NZ * NG, T), 0)
        return (((q >> 1) & 3) * NZ + (q >> 3)) * NC + (q & 1)

    def send_meta():
        ids = expert_of_row()
        hit_sum = jnp.zeros((NZ * NG, T), F32)
        prob_sum = jnp.zeros((NZ * NG, T), F32)
        for k in range(TOP):
            hit = ids == routes_t[k : k + 1, :]
            hit_sum = hit_sum + jnp.where(hit, 1.0, 0.0)
            prob_sum = prob_sum + jnp.where(hit, probs_t[k : k + 1, :].astype(F32), 0.0)
        before = jnp.where(iota((T, T), 0) < iota((T, T), 1), 1.0, 0.0).astype(BF16)
        rank = hit_sum * (nn(hit_sum.astype(BF16), before) + 1.0)
        for d in range(NZ):
            part = slice(d * NG, (d + 1) * NG)
            meta_out[d] = jnp.concatenate([rank[part], prob_sum[part]], axis=0).astype(BF16)
        for d in range(1, NZ):
            m_copy(d).start()
        meta_in[z] = meta_out[z]

    def permute_slots():
        def some(cg, carry):
            n = cg * 256 + iota((1, 256), 1)
            g, r = n >> 7, n & 127
            zr = div13(r)
            slot = (((g >> 1) * NZ + zr) * NC + (g & 1)) * CAP + (r - zr * CAP)
            slot = jnp.where(r < NZ * CAP, slot, -1)
            perm = jnp.where(iota((NG * NZ * CAP, 256), 0) == slot, 1.0, 0.0).astype(BF16)
            cols = pl.ds(pl.multiple_of(cg * 256, 256), 256)
            for j in range(NX):
                gp[j, :, cols] = nn(gpre[pl.ds(j * HS, HS), :], perm).astype(BF16)
                up[j, :, cols] = nn(upre[pl.ds(j * HS, HS), :], perm).astype(BF16)
            return carry

        lax.fori_loop(0, S // 256, some, 0)

    def build_tables():
        for d in range(1, NZ):
            m_copy(d).wait()
        table = jnp.concatenate([meta_in[d].astype(F32) for d in range(NZ)], axis=1)
        r = iota((GR, NZ * T), 0)
        zr = div13(r)
        key = jnp.where(
            (zr == (iota((GR, NZ * T), 1) >> 7)) & (r < NZ * CAP), r - zr * CAP + 1, -1
        ).astype(F32)
        for g in range(NG):
            oh[g] = jnp.where(table[g : g + 1, :] == key, 1.0, 0.0).astype(BF16)
        table16 = table.astype(BF16)
        for g in range(NG):
            rows = nt(table16, oh[g])
            ws[g] = jnp.broadcast_to(rows[NG + g : NG + g + 1, :], (16, GR)).astype(BF16)
        for i in range(7):
            w_copy(i).start()
        wr[me_g] = ws[me_g]

    def transpose_tables():
        for g in range(NG):
            oht[:, pl.ds(g * GR, GR)] = oh[g].T

    def slot_weight():
        return jnp.concatenate([wr[g][0:1, :].astype(F32) for g in range(NG)], axis=1)

    def activation(j):
        gate_val, up_val = gp[j].astype(F32), up[j].astype(F32)
        logistic = 1.0 / (1.0 + jnp.exp(-gate_val))
        silu = gate_val * logistic
        return gate_val, up_val, logistic, silu, (silu * up_val).astype(BF16).astype(F32)

    def tile_act(j):
        aw[j] = (slot_weight() * activation(j)[4]).astype(BF16)

    def tile_back(j):
        back = jnp.zeros((HS, S), F32)
        for k in range(NK):
            cols = pl.ds(k * CW, CW)
            back = back + nt(wfull[DOWN, j, :, cols], slots[0, :, :, cols].reshape(S, CW))
        gate_val, up_val, logistic, silu, act = activation(j)
        total = jnp.sum(back * act, axis=0, keepdims=True)
        if j == 0:
            psum[0:1, :] = total
        else:
            psum[0:1, :] = psum[0:1, :] + total
        scaled = slot_weight() * back
        gp[j] = (scaled * up_val * logistic * (1.0 + gate_val * (1.0 - logistic))).astype(BF16)
        up[j] = (scaled * silu).astype(BF16)

    parts = (pt0, wfull.at[DOWN], pt2)
    lefts = (aw, gp, up)

    def rs_copy(a, k, i):
        p, cols = parts[a], pl.ds(k * CW, CW)
        sign = 1 if k % 2 == 0 else -1
        if i == 0:
            src, dst, device = p.at[at_x(2), :, cols], xrel.at[a, :, cols], dev_x(sign)
        elif i == 1:
            src, dst, device = p.at[at_x(-sign), :, cols], xfin.at[a, 1, :, cols], dev_x(-sign)
        else:
            src, dst, device = p.at[at_x(sign), :, cols], xfin.at[a, 0, :, cols], dev_x(sign)
        return remote(src, dst, rs_s.at[a, k, i], rs_r.at[a, k, i], device)

    def part(a, k):
        cols = pl.ds(k * CW, CW)
        for j in range(NX):
            rows = nn(lefts[a][j], slots[min(a, 1), :, :, cols].reshape(S, CW))
            parts[a][j, :, cols] = rows.astype(BF16)
        rs_copy(a, k, 0).start()
        rs_copy(a, k, 1).start()

    def rs_relay(a, k):
        p, cols = parts[a], pl.ds(k * CW, CW)
        to = at_x(1 if k % 2 == 0 else -1)
        rs_copy(a, k, 0).wait_recv()
        p[to, :, cols] = (p[to, :, cols].astype(F32) + xrel[a, :, cols].astype(F32)).astype(BF16)
        rs_copy(a, k, 2).start()

    def out_copy(a, k):
        cols = pl.ds(k * CW, CW)
        return pltpu.make_async_copy(
            stage.at[:, cols], (dg, gg, ug)[a].at[:, cols], out_sem.at[a, k]
        )

    def rs_finish(a, k):
        cols = pl.ds(k * CW, CW)
        rs_copy(a, k, 1).wait_recv()
        rs_copy(a, k, 2).wait_recv()
        if a != DOWN:
            out_copy(a - 1, k).wait()
        total = xfin[a, 0, :, cols].astype(F32) + xfin[a, 1, :, cols].astype(F32)
        stage[:, cols] = parts[a][x, :, cols].astype(F32) + total
        out_copy(a, k).start()
        for i in range(3):
            rs_copy(a, k, i).wait_send()

    def yr_copy(k, i):
        col, width = BACK[k]
        g, device = dev_y(i)
        return remote(
            ys.at[TURN[NT + k] % NYS, g, pl.ds(0, GS), pl.ds(0, width)],
            zb.at[0, me_g, pl.ds(0, GS), pl.ds(col, width)],
            yr_s.at[k, i], yr_r.at[k, i], device,
        )

    def give_back(k):
        col, width = BACK[k]
        cols, slot = pl.ds(col, width), TURN[NT + k] % NYS
        free_buffer(NT + k)
        rows = nn(gbt[...], wfull[GATE, :, :, cols].reshape(H, width))
        rows = rows + nn(ubt[...], wfull[UP, :, :, cols].reshape(H, width))
        ys[slot, :, :, pl.ds(0, width)] = rows.astype(BF16).reshape(NG, GR, width)
        for i in range(7):
            yr_copy(k, i).start()
        zb[0, me_g, :, cols] = ys[slot, me_g, :, pl.ds(0, width)]

    def tz_copy(k, way, s):
        cols = pl.ds(*BACK[k])
        sign = 1 if way == 0 else -1
        count = hops(k)[way]
        i = s if way == 0 else hops(k)[0] + s
        return remote(
            zb.at[1, at_z(sign * (count - s)), :, cols], zrecv.at[i, :, cols],
            tz_s.at[k, i], tz_r.at[k, i], dev_z(sign),
        )

    def combine(k):
        col, width = BACK[k]
        cols = pl.ds(col, width)
        for i in range(7):
            yr_copy(k, i).wait_recv()
        total = nn(oht[...], zb[0, :, :, cols].reshape(S, width))
        zb[1, :, :, cols] = total.astype(BF16).reshape(NZ, T, width)

    def tz_step(k, s):
        cols = pl.ds(*BACK[k])
        if s == 0:
            combine(k)
        for way in range(2):
            sign, count = (1 if way == 0 else -1), hops(k)[way]
            base = 0 if way == 0 else hops(k)[0]
            if 1 <= s <= count:
                tz_copy(k, way, s - 1).wait_recv()
            if s < count:
                if s >= 1:
                    to = at_z(sign * (count - s))
                    zb[1, to, :, cols] = (
                        zb[1, to, :, cols].astype(F32) + zrecv[base + s - 1, :, cols].astype(F32)
                    ).astype(BF16)
                tz_copy(k, way, s).start()
        if s == 4:
            first, second = hops(k)
            total = zb[1, z, :, cols].astype(F32) + zrecv[first - 1, :, cols].astype(F32)
            total = total + zrecv[first + second - 1, :, cols].astype(F32)
            dtok[:, cols] = total.astype(BF16)

    def send_probs():
        for g in range(NG):
            ps[g] = jnp.broadcast_to(psum[0:1, pl.ds(g * GR, GR)], (16, GR)).astype(BF16)
        for i in range(7):
            p_copy(i).start()
        pr[me_g] = ps[me_g]

    def transpose_backs():
        for g in range(NG):
            cols = pl.ds(g * GR, GR)
            gbt[cols, :] = gp[:, :, cols].reshape(H, GR).T
            ubt[cols, :] = up[:, :, cols].reshape(H, GR).T

    def return_probs():
        for i in range(7):
            p_copy(i).wait()
        dense = jnp.concatenate([nn(pr[g], oh[g])[0:1, :] for g in range(NG)], axis=0)
        for d in range(NZ):
            some = dense[:, d * T : (d + 1) * T]
            dps[d] = jnp.concatenate([some, jnp.zeros((16 - NG, T), F32)], axis=0).astype(BF16)
        for d in range(1, NZ):
            q_copy(d).start()
        dpr[z] = dps[z]

    def pick_probs():
        for d in range(1, NZ):
            q_copy(d).wait()
        ids = expert_of_row()
        table = jnp.concatenate([dpr[d][0:NG, :].astype(F32) for d in range(NZ)], axis=0)
        rows = []
        for k in range(TOP):
            hit = ids == routes_t[k : k + 1, :]
            rows.append(jnp.sum(jnp.where(hit, table, 0.0), axis=0, keepdims=True))
        dprob[...] = jnp.concatenate(rows, axis=0).astype(BF16)

    zag_step(0, 0)
    send_meta()
    zag_step(1, 0)
    ag_start(0)
    ag_start(1)
    for a in range(2):
        slots[a, :, pl.ds(GS, GR - GS), :] = jnp.zeros((NG, GR - GS, D), BF16)

    for slot in range(1, NT + 4):
        for s in range(4, -1, -1):
            n = slot - s
            if 0 <= n < NT and (n, s) not in ((0, 0), (1, 0)):
                zag_step(n, s)
                if s == 4 and n < 7:
                    dispatch(n)
        if slot == 2:
            build_tables()
        if slot == 5:
            ag_relay(0)
            ag_start(2)
            ag_relay(1)
            permute_slots()
        if slot == 6:
            for i in range(7):
                w_copy(i).wait()
            for j in range(NX):
                tile_act(j)
        if slot == 7:
            ag_relay(2)
            arrived(0)
            arrived(1)
            part(DOWN, 0)
        if slot == 8:
            arrived(2)
            part(DOWN, 1)
            ag_finish(0)
        if slot == 9:
            arrived(3)
            part(DOWN, 2)
            transpose_tables()
        if slot == 10:
            arrived(4)
            part(DOWN, 3)
            tile_back(0)
            tile_back(1)
        if slot == 11:
            tile_back(2)
            tile_back(3)
            send_probs()
            transpose_backs()
            ag_finish(1)
            ag_finish(2)
            give_back(0)
            give_back(1)
            rs_relay(DOWN, 0)
    give_back(2)
    rs_relay(DOWN, 1)
    arrived(5)
    part(GATE, 0)
    part(UP, 0)
    rs_relay(DOWN, 2)
    dispatch(7)
    rs_relay(DOWN, 3)
    arrived(6)
    part(GATE, 1)
    part(UP, 1)
    return_probs()
    tz_step(0, 0)
    give_back(3)
    tz_step(0, 1)
    tz_step(1, 0)
    dispatch(8)
    rs_relay(GATE, 0)
    rs_relay(UP, 0)
    tz_step(0, 2)
    tz_step(1, 1)
    tz_step(2, 0)
    give_back(4)
    pick_probs()
    rs_relay(GATE, 1)
    rs_relay(UP, 1)
    tz_step(0, 3)
    tz_step(1, 2)
    tz_step(2, 1)
    arrived(7)
    part(GATE, 2)
    part(UP, 2)
    tz_step(0, 4)
    tz_step(1, 3)
    tz_step(2, 2)
    tz_step(3, 0)
    for k in range(NK):
        rs_finish(DOWN, k)
    tz_step(1, 4)
    tz_step(2, 3)
    tz_step(3, 1)
    rs_relay(GATE, 2)
    rs_relay(UP, 2)
    tz_step(2, 4)
    tz_step(3, 2)
    arrived(8)
    part(GATE, 3)
    part(UP, 3)
    tz_step(3, 3)
    tz_step(4, 0)
    for k in range(2):
        rs_finish(GATE, k)
        rs_finish(UP, k)
    tz_step(3, 4)
    tz_step(4, 1)
    rs_relay(GATE, 3)
    rs_relay(UP, 3)
    tz_step(4, 2)
    rs_finish(GATE, 2)
    rs_finish(UP, 2)
    tz_step(4, 3)
    tz_step(4, 4)
    rs_finish(GATE, 3)
    rs_finish(UP, 3)
    for k in range(NB):
        for way in range(2):
            for s in range(hops(k)[way]):
                tz_copy(k, way, s).wait_send()
    for chunk in ORDER[-NYS:]:
        sent(chunk)
    for k in range(NK):
        out_copy(UP, k).wait()


def hand_out(*refs):
    for i in range(5):
        refs[5 + i][...] = refs[i][...]


def on_device(
    d_out, saved_input, routes, probs, gate_pre, up_pre, gate_weight, up_weight, down_weight
):
    any_space = pl.BlockSpec(memory_space=pl.ANY)
    vmem = pl.BlockSpec(memory_space=pltpu.VMEM)
    dma = pltpu.SemaphoreType.DMA
    weight_grad = jax.ShapeDtypeStruct((HS, D), F32)
    shapes = (
        jax.ShapeDtypeStruct((T, D), BF16),
        jax.ShapeDtypeStruct((TOP, T), BF16),
        weight_grad,
        weight_grad,
        weight_grad,
    )
    results = pl.pallas_call(
        body,
        out_shape=shapes,
        in_specs=[any_space] * 2 + [vmem] * 4 + [any_space] * 3,
        out_specs=(vmem, vmem, any_space, any_space, any_space),
        scratch_shapes=[
            pltpu.VMEM((3, NX, HS, D), BF16),
            pltpu.VMEM((2, NZ, T, D), BF16),
            pltpu.VMEM((NYS, NG, GR, CW), BF16),
            pltpu.VMEM((2, NG, GR, D), BF16),
            pltpu.VMEM((NG, GR, NZ * T), BF16),
            pltpu.VMEM((NZ * T, S), BF16),
            pltpu.VMEM((NX, HS, S), BF16),
            pltpu.VMEM((NX, HS, S), BF16),
            pltpu.VMEM((NX, HS, S), BF16),
            pltpu.VMEM((S, H), BF16),
            pltpu.VMEM((S, H), BF16),
            pltpu.VMEM((NX, HS, D), BF16),
            pltpu.VMEM((NX, HS, D), BF16),
            pltpu.VMEM((7, T, D), BF16),
            pltpu.VMEM((3, HS, D), BF16),
            pltpu.VMEM((3, 2, HS, D), BF16),
            pltpu.VMEM((HS, D), F32),
            pltpu.VMEM((8, S), F32),
        ]
        + [pltpu.VMEM((8, 16, T), BF16)] * 8
        + [dma((3, 4)), dma((3, 4)), dma((3, NK, 3)), dma((3, NK, 3))]
        + [dma((NT, 7)), dma((NT, 7)), dma((NB, 7)), dma((NB, 7))]
        + [dma((NT, 7)), dma((NT, 7)), dma((NB, 7)), dma((NB, 7))]
        + [dma((7,))] * 8
        + [dma((NT + 3,)), dma((3, NK))],
        compiler_params=pltpu.CompilerParams(
            collective_id=0, has_side_effects=True, vmem_limit_bytes=63 * 2**20
        ),
        cost_estimate=pl.CostEstimate(
            flops=16 * 10**9, bytes_accessed=20 * 10**6, transcendentals=10**6
        ),
    )(
        d_out, saved_input, routes.T, probs.T, gate_pre.T, up_pre.T,
        down_weight[0], gate_weight[0], up_weight[0],
    )
    half = D // 2
    whole = pl.BlockSpec((TOP, T), lambda i: (0, 0))
    token_part = pl.BlockSpec((T, half), lambda i: (0, i))
    weight_part = pl.BlockSpec((HS, half), lambda i: (0, i))
    blocks = (token_part, whole, weight_part, weight_part, weight_part)
    d_tokens, d_probs, down_grad, gate_grad, up_grad = pl.pallas_call(
        hand_out, grid=(2,), out_shape=shapes, in_specs=blocks, out_specs=blocks
    )(*results)
    return d_tokens, d_probs.T, gate_grad[None], up_grad[None], down_grad[None]


def solution(mesh):
    token = P(("rep", "ep"), None)
    weight = P("ep", "rep", None)
    return jax.shard_map(
        on_device,
        mesh=mesh,
        in_specs=(token,) * 6 + (weight,) * 3,
        out_specs=(token, token, weight, weight, weight),
        check_vma=False,
    )
```

time: 227 us -> 194 us (0.85); the launches traced: 226 us -> 191 us
  Pallas kernels: 217 us -> 190 us
  local copies, waits for them, and re-layouts: 8.84 us -> 0 us
    pallas_call x1 -> x2, Pallas kernels: 217 us -> 190 us  [the longest x1 186 us: on_device(): pl.pallas_call(body, out_shape=shapes, in_specs=[any_space] * 2 + [vmem]...]
    unnamed x9 -> x0, local copies, waits for them, and re-layouts: 8.84 us -> none
where the time goes in v2:
time: 194 us; the launch traced here: 191 us
  Pallas kernels  190 us (98%)
    pallas_call x1, Pallas kernels, on_device(): pl.pallas_call(body, out_shape=shapes, in_specs=[any_space] * 2 + [vmem]...  186 us
    pallas_call x1, Pallas kernels, on_device(): pl.pallas_call(hand_out, grid=(2,), out_shape=shapes, in_specs=blocks, ou...  4.1 us

profile of v2, /device:TPU:6, one launch (start us, length us, event | category | flops | bytes accessed | tf_op | source)
XLA Modules:
  0.0 190.6 jit_solution(4437968240887710363)
XLA Ops:
  0.6 185.6 %shard_map.128 = (bf16[128,2048]{1,0:T(8,128)(2,1)}, bf16[6,128]{1,0:T(8,128)(2,1)}, f32[176,2048]{1,0:T(8,128)}, f32[176,2048]{1,0:T(8,128)}, f32[176,2048]{1,0:T(8,128)}) custom-call(bf16[128,2048]{1,0:T(8,128)(2,1)} %d_out.1, bf16[128,2048]{1,0:T(8,128)(2,1)} %saved.1, s32[6,128]{1,0:T(8,128)} %bitcast.19, bf16[6,128]{1,0:T(8,128)(2,1)} %bitcast.20, ...), custom_call_target="tpu_custom_call" | custom-call | flops 16000000000 | bytes 20000000 | tf_op jit(solution)/shard_map/pallas_call | solution.py:576
  186.3 4.1 %shard_map.129 = (bf16[128,2048]{1,0:T(8,128)(2,1)}, bf16[6,128]{1,0:T(8,128)(2,1)}, f32[176,2048]{1,0:T(8,128)}, f32[176,2048]{1,0:T(8,128)}, f32[176,2048]{1,0:T(8,128)}) custom-call(bf16[128,2048]{1,0:T(8,128)(2,1)} %get-tuple-element.15.refs_0_, bf16[6,128]{1,0:T(8,128)(2,1)} %get-tuple-element.16.refs_1_, f32[176,2048]{1,0:T(8,128)} %get-tuple-element.17.refs_2_, ...), custom_call_target="tpu_custom_call" | custom-call | tf_op jit(solution)/shard_map/pallas_call | solution.py:622

commit v3 on v2

--- a/solution.py
+++ b/solution.py
@@ -13,11 +13,11 @@
 HS = H // NX
 NK = 4
 CW = D // NK
-THERE = [(0, 0, 256), (0, 256, 256), (0, 512, 512), (0, 1024, 512), (0, 1536, 512)]
+THERE = [(0, 0, 512), (0, 512, 512), (0, 1024, 512), (0, 1536, 512)]
 THERE += [(1, 0, 512), (1, 512, 512), (1, 1024, 512), (1, 1536, 512)]
 BACK = [(0, 512), (512, 512), (1024, 512), (1536, 256), (1792, 256)]
 NT, NB, NYS = len(THERE), len(BACK), 4
-ORDER = [0, 1, 2, 3, 4, 5, 6, NT, NT + 1, NT + 2, 7, NT + 3, 8, NT + 4]
+ORDER = [0, 1, 2, 3, 4, 5, NT, NT + 1, NT + 2, 6, NT + 3, 7, NT + 4]
 TURN = {chunk: place for place, chunk in enumerate(ORDER)}
 GR = 128
 GS = 112
@@ -26,7 +26,7 @@
 DOWN, GATE, UP = 0, 1, 2
 MESH = pl.DeviceIdType.MESH
 F32, BF16 = jnp.float32, jnp.bfloat16
-Y_OFFSETS = [(dy, dc) for dy in range(NY) for dc in range(NC) if (dy, dc) != (0, 0)]
+Y_OFFSETS = [(2, 0), (1, 0), (3, 0), (2, 1), (1, 1), (3, 1), (0, 1)]
 
 
 def nn(a, b):
@@ -438,39 +438,38 @@
             n = slot - s
             if 0 <= n < NT and (n, s) not in ((0, 0), (1, 0)):
                 zag_step(n, s)
-                if s == 4 and n < 7:
+                if s == 4 and n < 6:
                     dispatch(n)
         if slot == 2:
             build_tables()
-        if slot == 5:
+        if slot == 4:
             ag_relay(0)
             ag_start(2)
             ag_relay(1)
             permute_slots()
-        if slot == 6:
+        if slot == 5:
             for i in range(7):
                 w_copy(i).wait()
             for j in range(NX):
                 tile_act(j)
-        if slot == 7:
+        if slot == 6:
             ag_relay(2)
             arrived(0)
+            part(DOWN, 0)
+        if slot == 7:
             arrived(1)
-            part(DOWN, 0)
+            part(DOWN, 1)
+            ag_finish(0)
         if slot == 8:
             arrived(2)
-            part(DOWN, 1)
-            ag_finish(0)
+            part(DOWN, 2)
+            transpose_tables()
         if slot == 9:
             arrived(3)
-            part(DOWN, 2)
-            transpose_tables()
-        if slot == 10:
-            arrived(4)
             part(DOWN, 3)
             tile_back(0)
             tile_back(1)
-        if slot == 11:
+        if slot == 10:
             tile_back(2)
             tile_back(3)
             send_probs()
@@ -482,13 +481,13 @@
             rs_relay(DOWN, 0)
     give_back(2)
     rs_relay(DOWN, 1)
-    arrived(5)
+    arrived(4)
     part(GATE, 0)
     part(UP, 0)
     rs_relay(DOWN, 2)
-    dispatch(7)
+    dispatch(6)
     rs_relay(DOWN, 3)
-    arrived(6)
+    arrived(5)
     part(GATE, 1)
     part(UP, 1)
     return_probs()
@@ -496,7 +495,7 @@
     give_back(3)
     tz_step(0, 1)
     tz_step(1, 0)
-    dispatch(8)
+    dispatch(7)
     rs_relay(GATE, 0)
     rs_relay(UP, 0)
     tz_step(0, 2)
@@ -509,7 +508,7 @@
     tz_step(0, 3)
     tz_step(1, 2)
     tz_step(2, 1)
-    arrived(7)
+    arrived(6)
     part(GATE, 2)
     part(UP, 2)
     tz_step(0, 4)
@@ -525,7 +524,7 @@
     rs_relay(UP, 2)
     tz_step(2, 4)
     tz_step(3, 2)
-    arrived(8)
+    arrived(7)
     part(GATE, 3)
     part(UP, 3)
     tz_step(3, 3)

time: 194 us -> 192 us (0.990)
  Pallas kernels: 190 us -> 187 us
    pallas_call x1, Pallas kernels: 186 us -> 183 us  [on_device(): pl.pallas_call(body, out_shape=shapes, in_specs=[any_space] * 2 + [vmem]...]
where the time goes in v3:
time: 192 us; the launch traced here: 188 us
  Pallas kernels  187 us (97%)
    pallas_call x1, Pallas kernels, on_device(): pl.pallas_call(body, out_shape=shapes, in_specs=[any_space] * 2 + [vmem]...  183 us
    pallas_call x1, Pallas kernels, on_device(): pl.pallas_call(hand_out, grid=(2,), out_shape=shapes, in_specs=blocks, ou...  4.1 us

profile of v3, /device:TPU:6, one launch (start us, length us, event | category | flops | bytes accessed | tf_op | source)
XLA Modules:
  0.0 188.4 jit_solution(3777042341579771684)
XLA Ops:
  0.6 183.2 %shard_map.128 = (bf16[128,2048]{1,0:T(8,128)(2,1)}, bf16[6,128]{1,0:T(8,128)(2,1)}, f32[176,2048]{1,0:T(8,128)}, f32[176,2048]{1,0:T(8,128)}, f32[176,2048]{1,0:T(8,128)}) custom-call(bf16[128,2048]{1,0:T(8,128)(2,1)} %d_out.1, bf16[128,2048]{1,0:T(8,128)(2,1)} %saved.1, s32[6,128]{1,0:T(8,128)} %bitcast.19, bf16[6,128]{1,0:T(8,128)(2,1)} %bitcast.20, ...), custom_call_target="tpu_custom_call" | custom-call | flops 16000000000 | bytes 20000000 | tf_op jit(solution)/shard_map/pallas_call | solution.py:575
  183.8 4.1 %shard_map.129 = (bf16[128,2048]{1,0:T(8,128)(2,1)}, bf16[6,128]{1,0:T(8,128)(2,1)}, f32[176,2048]{1,0:T(8,128)}, f32[176,2048]{1,0:T(8,128)}, f32[176,2048]{1,0:T(8,128)}) custom-call(bf16[128,2048]{1,0:T(8,128)(2,1)} %get-tuple-element.15.refs_0_, bf16[6,128]{1,0:T(8,128)(2,1)} %get-tuple-element.16.refs_1_, f32[176,2048]{1,0:T(8,128)} %get-tuple-element.17.refs_2_, ...), custom_call_target="tpu_custom_call" | custom-call | tf_op jit(solution)/shard_map/pallas_call | solution.py:621
